TPU v7x, 256 devices: a whole 4x4x8 slice. The times are simulated.
256 devices in a mesh: row: 16 (over z_hi, y, core), col: 4 (over z_lo), depth: 4 (over x).
Axes of the slice: x: 4, y: 4, z: 8 (z_hi: 2, z_lo: 4; z = z_hi * 4 + z_lo), core: 2. Of those that a mesh axis runs over, the one named last changes fastest.
Arguments:
- packed: bfloat16 [1024, 128, 128], P(('row', 'col', 'depth')), may hold values from -6 to 6
- block_index: int32 [8, 256], replicated, may hold values from 0 to 1023, as said below
- block_sign: int32 [8, 256], replicated, may hold values from -1 to 1, as said below
- ovov: bfloat16 [32768, 32768], P('row', ('col', 'depth')), may hold values from -0.03125 to 0.03125
- residual_in: bfloat16 [1024, 32768], P('row', ('col', 'depth')), may hold values from -6 to 6
Outputs:
- updated: bfloat16 [1024, 32768], P('row', ('col', 'depth'))
Inputs may be any that keep to these rules, and one draw needn't show every extreme that they name: `block_index`: each packed block is named by exactly two entries. Entries in block column s name packed blocks from (s // 16) * 8 * 8 to (s // 16 + 1) * 8 * 8 - 1. `block_sign`: every entry is 1 or -1; the two entries that name one packed block have opposite signs.
All inputs are finite; a program needn't handle non-finite values.
Results may differ from a plain program's by a relative error of at most 0.001.
Values may be sent and summed in bfloat16 or wider, within the bound.
A program may use at most 64 MiB of HBM per device.

v0:
```python
import jax
import jax.numpy as jnp
from jax import lax
from jax.sharding import PartitionSpec as P


def per_device(packed, block_index, block_sign, ovov, residual_in):
    block_size = packed.shape[1]
    row_blocks = block_index.shape[0]
    col_blocks = ovov.shape[0] // block_size
    group_blocks = row_blocks * col_blocks // 2
    group_index = lax.axis_index("row")
    index_mine = (
        lax.dynamic_slice_in_dim(block_index, group_index * col_blocks, col_blocks, 1)
        - group_index * group_blocks
    )
    sign_mine = lax.dynamic_slice_in_dim(block_sign, group_index * col_blocks, col_blocks, 1)
    flat_index = index_mine.reshape(-1)
    flat_sign = sign_mine.reshape(-1).astype(jnp.float32)
    piece = lax.all_gather(packed, ("col", "depth"), axis=0, tiled=True)
    count = piece.shape[0]
    slots = jnp.arange(count, dtype=jnp.int32)
    select = jnp.where(flat_index[:, None] == slots[None, :], flat_sign[:, None], 0.0).astype(
        jnp.bfloat16
    )
    added = jnp.dot(
        select, piece.reshape(count, block_size * block_size), preferred_element_type=jnp.float32
    )
    blocks = added.astype(jnp.bfloat16)
    slab = blocks.reshape(row_blocks, col_blocks, block_size, block_size).transpose(0, 2, 1, 3)
    slab = slab.reshape(row_blocks * block_size, col_blocks * block_size)
    share_rows = residual_in.shape[0]
    totals = lax.psum(jnp.dot(slab, ovov, preferred_element_type=jnp.float32), "row")
    mine = lax.dynamic_slice_in_dim(totals, group_index * share_rows, share_rows, 0)
    return (residual_in.astype(jnp.float32) + mine).astype(jnp.bfloat16)


def solution(mesh):
    in_specs = (
        P(("row", "col", "depth"), None, None),
        P(),
        P(),
        P("row", ("col", "depth")),
        P("row", ("col", "depth")),
    )
    out_specs = P("row", ("col", "depth"))
    return jax.shard_map(
        per_device, mesh=mesh, in_specs=in_specs, out_specs=out_specs, check_vma=False
    )
```

profile of v0, /device:TPU:1, one launch (start us, length us, event | category | flops | bytes accessed | tf_op | source)
XLA Modules:
  0.0 352.5 jit_solution(893513759422192371)
XLA Ops:
  6.5 0.0 all-gather.2.cloned.1.call-start
  6.5 0.7 all-gather.2.cloned.1.call-update
  7.3 0.0 all-reduce.2.cloned.1.call-start
  7.3 0.8 dynamic-slice_convert_fusion
  8.1 0.1 convert_element_type.24
  8.2 0.1 eq.15
  8.3 78.4 %all-gather.2.cloned.1.call-done = bf16[64,128,128]{2,1,0:T(8,128)(2,1)} async-done(((bf16[4,128,128]{2,1,0:T(8,128)(2,1)}), bf16[64,128,128]{2,1,0:T(8,128)(2,1)}) %all-gather.2.cloned.1.call-update) | async-done | bytes 2097168 | tf_op jit(solution)/shard_map/all_gather | solution.py:20
  86.6 3.3 fusion.3
  90.0 0.0 slice-start
  90.0 1.2 copy.9
  91.2 0.0 slice-start.1
  91.2 2.7 copy.7
  93.9 0.0 slice-done
  94.0 0.0 slice-done.1
  94.0 11.2 %fusion = f32[1024,2048]{1,0:T(8,128)} fusion(bf16[2048,2048]{1,0:T(8,128)(2,1)S(1)} %bitcast.19, bf16[128,8,16,128]{3,2,1,0:T(8,128)(2,1)S(1)} %bitcast.16), kind=kOutput, calls=%fused_computation.1 | convolution fusion | flops 8589934592 | bytes 20971520 | tf_op jit(solution)/shard_map/dot_general | solution.py:33
  105.1 0.0 copy-start
  105.2 0.0 all-reduce.2.cloned.1.call-update
  105.2 238.7 %all-reduce.2.cloned.1.call-done = f32[1024,2048]{1,0:T(8,128)} async-done(((f32[1024,2048]{1,0:T(8,128)}), f32[1024,2048]{1,0:T(8,128)}) %all-reduce.2.cloned.1.call-update) | async-done | bytes 8388624 | tf_op jit(solution)/shard_map/psum | solution.py:33
  343.8 0.0 copy-done
  343.8 1.8 add_convert_fusion
  (1 shorter events, 0.0 us)
Async XLA Ops:
  6.5 80.1 %all-gather.2.cloned.1.call-start = ((), (), s32[]{:S(2)}) async-start(), calls=%async_computation | async-start | bytes 2228224 | tf_op jit(solution)/shard_map/all_gather | solution.py:20
  7.3 336.6 %all-reduce.2.cloned.1.call-start = ((), (), s32[]{:S(2)}) async-start(), calls=%async_computation.1 | async-start | bytes 16777216 | tf_op jit(solution)/shard_map/psum | solution.py:33
  90.0 4.0 %slice-start = ((s8[8388608]{0:T(1024)(128)(4,1)}), s8[4194304]{0:T(1024)(128)(4,1)S(1)}, s32[]{:S(2)}) async-start(s8[8388608]{0:T(1024)(128)(4,1)} %bitcast.18), calls=%async_computation.2 | async-start | bytes 8388608
  91.2 2.7 slice-start.1
  105.1 238.7 %copy-start = (bf16[64,2048]{1,0:T(8,128)(2,1)S(1)}, bf16[64,2048]{1,0:T(8,128)(2,1)}, u32[]{:S(2)}) copy-start(bf16[64,2048]{1,0:T(8,128)(2,1)} %param.9) | copy-start | bytes 786436
Sparse Core Ops, SparseCore 0:
  9.1 77.4 all-gather.1
  105.3 238.4 all-reduce.1
where the time goes:
time: 353 us; the launch traced here: 352 us
  waiting for transfers between devices  318 us (90%)
  matrix products  14.5 us (4%)
  between operations  13.5 us (4%)
  local copies, waits for them, and re-layouts  4.14 us (1%)
    psum x1, waiting for transfers between devices, per_device(): lax.psum(jnp.dot(slab, ovov, preferred_element_type=jnp.float32), 'row')  239 us
    all_gather x1, waiting for transfers between devices, per_device(): piece = lax.all_gather(packed, ('col', 'depth'), axis=0, tiled=True)  78.4 us
    dot_general x1, matrix products, per_device(): jnp.dot(slab, ovov, preferred_element_type=jnp.float32)  11.2 us
  transfers between devices with their start and end apart: 2, of which 2 were waited for; matrix products, arithmetic and copies ran while one was open for 0% of the time, Pallas kernels for 0%

commit v1 on v0

v1 whole, which is shorter than its diff:
```python
import math

import jax
import jax.numpy as jnp
from jax import lax
from jax.experimental import pallas as pl
from jax.experimental.pallas import tpu as pltpu
from jax.sharding import PartitionSpec as P

MESH = pl.DeviceIdType.MESH
F32 = jnp.float32
BF16 = jnp.bfloat16
I16 = jnp.int16
I32 = jnp.int32

NY, NX, NZ = 4, 4, 4
BLOCK = 128
HALVES = 8
XF = 6
PANELS = 2
PW = 1024
MW = 512
SHARE = 64
TILES = MW // 128
MROWS = SHARE * TILES + 16
STEPS = 64.0
TOP = 32000.0
LN2 = math.log(2.0)


def encode(tiles):
    split = [t.reshape(SHARE // 16, 16, 128) for t in tiles]
    top = jnp.max(jnp.abs(split[0]), axis=0)
    for t in split[1:]:
        top = jnp.maximum(top, jnp.max(jnp.abs(t), axis=0))
    code = jnp.ceil(jnp.log(jnp.maximum(top, 1e-30)) * (STEPS / LN2)) + 1.0
    inverse = jnp.exp(code * (-LN2 / STEPS)) * TOP
    values = [
        jnp.round(t * inverse[None]).astype(I32).astype(I16).reshape(SHARE, 128) for t in split
    ]
    return values, code.astype(I32).astype(I16)


def decode(ref):
    code = ref[pl.ds(SHARE * TILES, 16), :].astype(I32).astype(F32)
    scale = jnp.exp(code * (LN2 / STEPS)) * (1.0 / TOP)
    out = []
    for t in range(TILES):
        v = ref[pl.ds(t * SHARE, SHARE), :].astype(I32).astype(F32)
        out.append((v.reshape(SHARE // 16, 16, 128) * scale[None]).reshape(SHARE, 128))
    return out


def add(a, b):
    return [x + y for x, y in zip(a, b)]


def kernel(
    index_ref, sign_ref, packed_ref, ovov_ref, residual_ref, out_ref,
    gath, ovov, resid, slab, acc, d2d, msend, mrecv,
    local_sem, gs, gr, ds, dr, ms, mr,
):
    row = lax.axis_index("row")
    col = lax.axis_index("col")
    dep = lax.axis_index("depth")
    core = lax.rem(row, 2)
    y = lax.rem(row // 2, NY)
    zh = row // (2 * NY)

    def row_of(zh_, y_, core_):
        return (zh_ * NY + y_) * 2 + core_

    sibling = {"row": row_of(zh, y, 1 - core)}
    y_up = {"row": row_of(zh, lax.rem(y + 1, NY), core)}
    y_down = {"row": row_of(zh, lax.rem(y + NY - 1, NY), core)}
    z_far = {"row": row_of(1 - zh, y, core)}
    dep_up, dep_down = lax.rem(dep + 1, NX), lax.rem(dep + NX - 1, NX)
    dep_far = lax.rem(dep + 2, NX)
    x_up, x_down = {"depth": dep_up}, {"depth": dep_down}
    z_up = {"row": row_of(lax.rem(zh + (col + 1) // NZ, 2), y, core), "col": lax.rem(col + 1, NZ)}
    z_down = {
        "row": row_of(lax.rem(zh + 1 + (col + NZ - 1) // NZ, 2), y, core),
        "col": lax.rem(col + NZ - 1, NZ),
    }

    def slot(c, d):
        return (c * NX + d) * HALVES

    mine = slot(col, dep)
    own_copy = pltpu.make_async_copy(packed_ref, gath.at[pl.ds(mine, HALVES)], local_sem.at[0])
    own_copy.start()
    res_copy = pltpu.make_async_copy(residual_ref, resid, local_sem.at[1])
    ovov_copy = pltpu.make_async_copy(ovov_ref, ovov, local_sem.at[2])
    ovov_copy.start()
    res_copy.start()

    barrier = pltpu.get_barrier_semaphore()
    peers = (sibling, y_up, y_down, z_far, x_up, x_down, z_up, z_down)
    for p in peers:
        pl.semaphore_signal(barrier, inc=1, device_id=p, device_id_type=MESH)
    pl.semaphore_wait(barrier, len(peers))
    own_copy.wait()

    sends = []

    def guarded(cond, fn):
        if cond is None:
            fn()
        else:
            pl.when(cond)(fn)

    def send(cond, first, count, sem, target):
        part = gath.at[pl.ds(first, count)]
        number = len(sends)
        copy = pltpu.make_async_remote_copy(
            part, part, gs.at[number], gr.at[sem], device_id=target, device_id_type=MESH
        )
        sends.append((cond, copy))
        guarded(cond, copy.start)

    def arrive(cond, first, count, sem):
        part = gath.at[pl.ds(first, count)]
        copy = pltpu.make_async_remote_copy(
            part, part, gs.at[0], gr.at[sem], device_id=sibling, device_id_type=MESH
        )
        guarded(cond, copy.wait_recv)

    def sem_of(j, kind):
        return j * 8 + kind

    def both(a, b):
        return b if a is None else jnp.logical_and(a, b)

    can_up, can_down = col < NZ - 1, col > 0

    def rows_at(k):
        if k == 0:
            return [(None, col, 0)]
        return [(col >= k, col - k, 1), (col + k < NZ, col + k, -1)]

    def pass_on(cond, way, first, count, sem):
        if way >= 0:
            send(both(cond, can_up), first, count, sem, z_up)
        if way <= 0:
            send(both(cond, can_down), first, count, sem, z_down)

    def x_count(k):
        return HALVES if k == 0 else XF

    def step_share(k):
        for cond, j, way in rows_at(k):
            if k > 0:
                arrive(cond, slot(j, dep), HALVES, sem_of(j, 0))
            send(cond, slot(j, dep), x_count(k), sem_of(j, 1), x_up)
            send(cond, slot(j, dep), x_count(k), sem_of(j, 2), x_down)
            pass_on(cond, way, slot(j, dep), HALVES, sem_of(j, 0))

    def step_near(k):
        n = x_count(k)
        for cond, j, way in rows_at(k):
            arrive(cond, slot(j, dep_down), n, sem_of(j, 1))
            send(cond, slot(j, dep_down), n // 2, sem_of(j, 3), x_up)
            arrive(cond, slot(j, dep_up), n, sem_of(j, 2))
            send(cond, slot(j, dep_up) + n // 2, n // 2, sem_of(j, 4), x_down)

    rest = HALVES - XF

    def step_rest_near(k):
        for cond, j, way in rows_at(k):
            for kind, d in ((5, dep_down), (6, dep_up)):
                if k > 0:
                    arrive(cond, slot(j, d) + XF, rest, sem_of(j, kind))
                pass_on(cond, way, slot(j, d) + XF, rest, sem_of(j, kind))

    def step_far(k):
        n = x_count(k)
        for cond, j, way in rows_at(k):
            arrive(cond, slot(j, dep_far), n // 2, sem_of(j, 3))
            arrive(cond, slot(j, dep_far) + n // 2, n // 2, sem_of(j, 4))
            if k > 0:
                arrive(cond, slot(j, dep_far) + XF, rest, sem_of(j, 7))
            pass_on(cond, way, slot(j, dep_far) + XF, rest, sem_of(j, 7))

    step_share(0)
    step_share(1)
    step_near(0)
    step_rest_near(0)
    step_share(2)
    step_near(1)
    step_far(0)
    step_rest_near(1)
    step_share(3)
    step_near(2)
    step_far(1)
    step_rest_near(2)
    step_near(3)
    step_far(2)
    step_rest_near(3)
    step_far(3)
    for cond, copy in sends:
        guarded(cond, copy.wait_send)
    ovov_copy.wait()

    def block_row(h, i):
        yy = lax.rem(y + (2, 1, NY - 1, 0)[i], NY)
        return ((1 - zh) if h == 0 else zh) * NY + yy

    blocks_per_row = ovov.shape[0] // BLOCK

    def build(h):
        for i in range(4):
            r = block_row(h, i)

            @pl.loop(0, blocks_per_row)
            def _(s):
                at = row * blocks_per_row + s
                p = lax.rem(index_ref[r, at], gath.shape[0] // 2)
                tile = gath[pl.ds(2 * p, 2)].reshape(BLOCK, BLOCK)
                sign = sign_ref[r, at].astype(F32)
                slab[pl.ds(i * BLOCK, BLOCK), pl.ds(pl.multiple_of(s * BLOCK, BLOCK), BLOCK)] = (
                    tile.astype(F32) * sign
                ).astype(BF16)

    my_rows = pl.ds(pl.multiple_of(core * SHARE, SHARE), SHARE)
    their_rows = pl.ds(pl.multiple_of((1 - core) * SHARE, SHARE), SHARE)
    units = [(h, q) for h in range(2) for q in range(PANELS)]
    NT = 256
    core_copies = []

    def multiply(u, part):
        h, q = units[u]

        @pl.loop(0, PW // NT)
        def _(n):
            here = pl.ds(pl.multiple_of(n * NT, NT), NT)
            there = pl.ds(pl.multiple_of(q * PW + n * NT, NT), NT)
            t = jnp.dot(
                slab[pl.ds(part * 256, 256), :], ovov[:, there], preferred_element_type=F32
            )
            for i in range(2):
                acc[u, part * 2 + i, :, here] = t[i * BLOCK : (i + 1) * BLOCK]

        copy = pltpu.make_async_remote_copy(
            acc.at[u, pl.ds(part * 2, 2), their_rows],
            d2d.at[u, pl.ds(part * 2, 2)],
            ds.at[u * 2 + part],
            dr.at[u * 2 + part],
            device_id=sibling,
            device_id_type=MESH,
        )
        copy.start()
        core_copies.append(copy)

    def summed(u, i, half):
        return [
            acc[u, i, my_rows, pl.ds(half * MW + t * 128, 128)]
            + d2d[u, i, :, pl.ds(half * MW + t * 128, 128)]
            for t in range(TILES)
        ]

    messages = {}

    def message_copy(number, target):
        return pltpu.make_async_remote_copy(
            msend.at[number], mrecv.at[number], ms.at[number], mr.at[number],
            device_id=target, device_id_type=MESH,
        )

    def post(number, tiles, target):
        values, code = encode(tiles)
        for t in range(TILES):
            msend[number, pl.ds(t * SHARE, SHARE), :] = values[t]
        msend[number, pl.ds(TILES * SHARE, 16), :] = code
        copy = message_copy(number, target)
        copy.start()
        messages[number] = copy

    def fetch(number):
        message_copy(number, sibling).wait_recv()
        return decode(mrecv.at[number])

    A, B = 0, 1
    def first_sends(u):
        core_copies[2 * u].wait_recv()
        post(u * 6 + 0, summed(u, 0, A), y_up)
        post(u * 6 + 1, summed(u, 0, B), y_down)
        post(u * 6 + 2, summed(u, 1, B), y_up)
        core_copies[2 * u + 1].wait_recv()
        post(u * 6 + 3, summed(u, 2, A), y_down)

    def second_sends(u):
        post(u * 6 + 4, add(summed(u, 1, A), fetch(u * 6 + 0)), y_up)
        post(u * 6 + 5, add(summed(u, 2, B), fetch(u * 6 + 1)), y_down)

    zbase = len(units) * 6

    def finish(u):
        h, q = units[u]
        total_a = add(add(summed(u, 3, A), fetch(u * 6 + 3)), fetch(u * 6 + 4))
        if h == 0:
            post(zbase + q * 2, total_a, z_far)
        else:
            store(q, A, add(total_a, fetch(zbase + q * 2)))
        total_b = add(add(summed(u, 3, B), fetch(u * 6 + 2)), fetch(u * 6 + 5))
        if h == 0:
            post(zbase + q * 2 + 1, total_b, z_far)
        else:
            store(q, B, add(total_b, fetch(zbase + q * 2 + 1)))

    def store(q, half, tiles):
        for t in range(TILES):
            at = pl.ds(q * PW + half * MW + t * 128, 128)
            out_ref[:, at] = (resid[:, at].astype(F32) + tiles[t]).astype(BF16)

    build(0)
    multiply(0, 0)
    multiply(0, 1)
    first_sends(0)
    multiply(1, 0)
    multiply(1, 1)
    second_sends(0)
    first_sends(1)
    build(1)
    multiply(2, 0)
    multiply(2, 1)
    finish(0)
    second_sends(1)
    first_sends(2)
    multiply(3, 0)
    multiply(3, 1)
    finish(1)
    second_sends(2)
    first_sends(3)
    second_sends(3)
    res_copy.wait()
    finish(2)
    finish(3)

    for copy in core_copies:
        copy.wait_send()
    for number in sorted(messages):
        messages[number].wait_send()


def per_device(packed, block_index, block_sign, ovov, residual_in):
    share, depth, width = packed.shape[0], ovov.shape[0], ovov.shape[1]
    plane = NZ * NX
    count = 4 * 6 + 4
    n_sends = 64
    anywhere = pl.BlockSpec(memory_space=pl.ANY)
    scalars = pl.BlockSpec(memory_space=pltpu.SMEM)
    return pl.pallas_call(
        kernel,
        out_shape=jax.ShapeDtypeStruct(residual_in.shape, BF16),
        in_specs=[scalars, scalars, anywhere, anywhere, anywhere],
        out_specs=pl.BlockSpec(memory_space=pltpu.VMEM),
        scratch_shapes=[
            pltpu.VMEM((plane * HALVES, BLOCK // 2, BLOCK), BF16),
            pltpu.VMEM((depth, width), BF16),
            pltpu.VMEM(residual_in.shape, BF16),
            pltpu.VMEM((4 * BLOCK, depth), BF16),
            pltpu.VMEM((4, 4, BLOCK, PW), F32),
            pltpu.VMEM((4, 4, SHARE, PW), F32),
            pltpu.VMEM((count, MROWS, 128), I16),
            pltpu.VMEM((count, MROWS, 128), I16),
            pltpu.SemaphoreType.DMA((3,)),
            pltpu.SemaphoreType.DMA((n_sends,)),
            pltpu.SemaphoreType.DMA((NZ * 8,)),
            pltpu.SemaphoreType.DMA((8,)),
            pltpu.SemaphoreType.DMA((8,)),
            pltpu.SemaphoreType.DMA((count,)),
            pltpu.SemaphoreType.DMA((count,)),
        ],
        compiler_params=pltpu.CompilerParams(
            collective_id=0, has_side_effects=True, vmem_limit_bytes=52 << 20
        ),
        cost_estimate=pl.CostEstimate(
            flops=2 * 1024 * depth * width, bytes_accessed=depth * width * 2, transcendentals=0
        ),
    )(
        block_index,
        block_sign,
        packed.reshape(share * 2, BLOCK // 2, BLOCK),
        ovov,
        residual_in,
    )


def solution(mesh):
    in_specs = (
        P(("row", "col", "depth"), None, None),
        P(),
        P(),
        P("row", ("col", "depth")),
        P("row", ("col", "depth")),
    )
    out_specs = P("row", ("col", "depth"))
    return jax.shard_map(
        per_device, mesh=mesh, in_specs=in_specs, out_specs=out_specs, check_vma=False
    )
```

time: 353 us -> 70.9 us (0.20)
  waiting for transfers between devices: 318 us -> 0 us
  Pallas kernels: 0 us -> 66.7 us
  matrix products: 14.5 us -> 0 us
  between operations: 13.5 us -> 0.01 us
    psum x1 -> x0, waiting for transfers between devices: 239 us -> none  [per_device(): lax.psum(jnp.dot(slab, ovov, preferred_element_type=jnp.float32), 'row')]
    all_gather x1 -> x0, waiting for transfers between devices: 78.4 us -> none  [per_device(): piece = lax.all_gather(packed, ('col', 'depth'), axis=0, tiled=True)]
    pallas_call x0 -> x1, Pallas kernels: none -> 66.7 us  [per_device(): pl.pallas_call(kernel, out_shape=jax.ShapeDtypeStruct(residual_in.shape,...]
    dot_general x2 -> x0, matrix products: 14.5 us -> none  [the longest x1 11.2 us: per_device(): jnp.dot(slab, ovov, preferred_element_type=jnp.float32)]
  transfers between devices with their start and end apart: 2 -> 0, of which waited for: 2 -> 0; matrix products, arithmetic and copies ran while one was open for 0% -> 0% of each run, Pallas kernels for 0% -> 0%
where the time goes in v1:
time: 70.9 us; the launch traced here: 70.7 us
  Pallas kernels  66.7 us (94%)
  local copies, waits for them, and re-layouts  3.95 us (6%)
    pallas_call x1, Pallas kernels, per_device(): pl.pallas_call(kernel, out_shape=jax.ShapeDtypeStruct(residual_in.shape,...  66.7 us
    unnamed x9, local copies, waits for them, and re-layouts  3.95 us

profile of v1, /device:TPU:1, one launch (start us, length us, event | category | flops | bytes accessed | tf_op | source)
XLA Modules:
  0.0 70.7 jit_solution(2102164277045118799)
XLA Ops:
  0.0 0.0 copy-start
  0.0 0.9 %copy-done = bf16[64,2048]{1,0:T(8,128)(2,1)S(1)} copy-done((bf16[64,2048]{1,0:T(8,128)(2,1)S(1)}, bf16[64,2048]{1,0:T(8,128)(2,1)}, u32[]{:S(2)}) %copy-start) | copy-done | bytes 262168
  1.0 0.0 copy-start.1
  1.0 0.9 %copy-done.1 = bf16[4,128,128]{2,1,0:T(8,128)(2,1)S(1)} copy-done((bf16[4,128,128]{2,1,0:T(8,128)(2,1)S(1)}, bf16[4,128,128]{2,1,0:T(8,128)(2,1)}, u32[]{:S(2)}) %copy-start.1) | copy-done | bytes 131096
  1.9 0.0 copy-start.2
  1.9 0.7 copy-done.2
  2.6 0.0 copy-start.3
  2.6 0.7 copy-done.3
  3.3 66.7 %shard_map.55 = bf16[64,2048]{1,0:T(8,128)(2,1)S(1)} custom-call(s32[8,256]{1,0:T(8,128)S(1)} %copy-done.2, s32[8,256]{1,0:T(8,128)S(1)} %copy-done.3, bf16[8,64,128]{2,1,0:T(8,128)(2,1)S(1)} %bitcast.1, bf16[2048,2048]{1,0:T(8,128)(2,1)} %ovov_ref.1, bf16[64,2048]{1,0:T(8,128)(2,1)S(1)} %copy-done), custom_call_target="tpu_custom_call" | custom-call | flops 8589934592 | bytes 8388608 | tf_op jit(solution)/shard_map/pallas_call | solution.py:352
  70.0 0.7 copy.7
Async XLA Ops:
  0.0 0.9 %copy-start = (bf16[64,2048]{1,0:T(8,128)(2,1)S(1)}, bf16[64,2048]{1,0:T(8,128)(2,1)}, u32[]{:S(2)}) copy-start(bf16[64,2048]{1,0:T(8,128)(2,1)} %residual_ref.1) | copy-start | bytes 786436
  1.0 0.9 %copy-start.1 = (bf16[4,128,128]{2,1,0:T(8,128)(2,1)S(1)}, bf16[4,128,128]{2,1,0:T(8,128)(2,1)}, u32[]{:S(2)}) copy-start(bf16[4,128,128]{2,1,0:T(8,128)(2,1)} %param.5) | copy-start | bytes 393220
  1.9 0.7 copy-start.2
  2.6 0.7 copy-start.3

commit v2 on v1

--- a/solution.py
+++ b/solution.py
@@ -56,8 +56,8 @@
 
 
 def kernel(
-    index_ref, sign_ref, packed_ref, ovov_ref, residual_ref, out_ref,
-    gath, ovov, resid, slab, acc, d2d, msend, mrecv,
+    index_hbm, sign_hbm, packed_ref, ovov_ref, residual_ref, out_ref,
+    index_ref, sign_ref, gath, ovov, resid, slab, acc, d2d, msend, mrecv,
     local_sem, gs, gr, ds, dr, ms, mr,
 ):
     row = lax.axis_index("row")
@@ -89,6 +89,10 @@
     mine = slot(col, dep)
     own_copy = pltpu.make_async_copy(packed_ref, gath.at[pl.ds(mine, HALVES)], local_sem.at[0])
     own_copy.start()
+    index_copy = pltpu.make_async_copy(index_hbm, index_ref, local_sem.at[3])
+    sign_copy = pltpu.make_async_copy(sign_hbm, sign_ref, local_sem.at[4])
+    index_copy.start()
+    sign_copy.start()
     res_copy = pltpu.make_async_copy(residual_ref, resid, local_sem.at[1])
     ovov_copy = pltpu.make_async_copy(ovov_ref, ovov, local_sem.at[2])
     ovov_copy.start()
@@ -200,12 +204,15 @@
     for cond, copy in sends:
         guarded(cond, copy.wait_send)
     ovov_copy.wait()
+    index_copy.wait()
+    sign_copy.wait()
 
     def block_row(h, i):
         yy = lax.rem(y + (2, 1, NY - 1, 0)[i], NY)
         return ((1 - zh) if h == 0 else zh) * NY + yy
 
     blocks_per_row = ovov.shape[0] // BLOCK
+    HALF = 4 * SHARE
 
     def build(h):
         for i in range(4):
@@ -215,48 +222,46 @@
             def _(s):
                 at = row * blocks_per_row + s
                 p = lax.rem(index_ref[r, at], gath.shape[0] // 2)
-                tile = gath[pl.ds(2 * p, 2)].reshape(BLOCK, BLOCK)
                 sign = sign_ref[r, at].astype(F32)
-                slab[pl.ds(i * BLOCK, BLOCK), pl.ds(pl.multiple_of(s * BLOCK, BLOCK), BLOCK)] = (
-                    tile.astype(F32) * sign
-                ).astype(BF16)
-
-    my_rows = pl.ds(pl.multiple_of(core * SHARE, SHARE), SHARE)
-    their_rows = pl.ds(pl.multiple_of((1 - core) * SHARE, SHARE), SHARE)
+                there = pl.ds(pl.multiple_of(s * BLOCK, BLOCK), BLOCK)
+                for part, c in ((0, 1 - core), (1, core)):
+                    tile = gath[2 * p + c]
+                    slab[pl.ds(part * HALF + i * SHARE, SHARE), there] = (
+                        tile.astype(F32) * sign
+                    ).astype(BF16)
+
     units = [(h, q) for h in range(2) for q in range(PANELS)]
-    NT = 256
     core_copies = []
 
     def multiply(u, part):
         h, q = units[u]
-
-        @pl.loop(0, PW // NT)
-        def _(n):
-            here = pl.ds(pl.multiple_of(n * NT, NT), NT)
-            there = pl.ds(pl.multiple_of(q * PW + n * NT, NT), NT)
-            t = jnp.dot(
-                slab[pl.ds(part * 256, 256), :], ovov[:, there], preferred_element_type=F32
+        acc[u, part] = jnp.dot(
+            slab[pl.ds(part * HALF, HALF), :],
+            ovov[:, pl.ds(q * PW, PW)],
+            preferred_element_type=F32,
+        )
+        if part == 1:
+            return
+        for w in range(2):
+            rows = pl.ds(w * 2 * SHARE, 2 * SHARE)
+            copy = pltpu.make_async_remote_copy(
+                acc.at[u, 0, rows],
+                d2d.at[u, rows],
+                ds.at[u * 2 + w],
+                dr.at[u * 2 + w],
+                device_id=sibling,
+                device_id_type=MESH,
             )
-            for i in range(2):
-                acc[u, part * 2 + i, :, here] = t[i * BLOCK : (i + 1) * BLOCK]
-
-        copy = pltpu.make_async_remote_copy(
-            acc.at[u, pl.ds(part * 2, 2), their_rows],
-            d2d.at[u, pl.ds(part * 2, 2)],
-            ds.at[u * 2 + part],
-            dr.at[u * 2 + part],
-            device_id=sibling,
-            device_id_type=MESH,
-        )
-        copy.start()
-        core_copies.append(copy)
+            copy.start()
+            core_copies.append(copy)
 
     def summed(u, i, half):
-        return [
-            acc[u, i, my_rows, pl.ds(half * MW + t * 128, 128)]
-            + d2d[u, i, :, pl.ds(half * MW + t * 128, 128)]
-            for t in range(TILES)
-        ]
+        rows = pl.ds(i * SHARE, SHARE)
+        out = []
+        for t in range(TILES):
+            at = pl.ds(half * MW + t * 128, 128)
+            out.append(acc[u, 1, rows, at] + d2d[u, rows, at])
+        return out
 
     messages = {}
 
@@ -348,22 +353,23 @@
     count = 4 * 6 + 4
     n_sends = 64
     anywhere = pl.BlockSpec(memory_space=pl.ANY)
-    scalars = pl.BlockSpec(memory_space=pltpu.SMEM)
     return pl.pallas_call(
         kernel,
         out_shape=jax.ShapeDtypeStruct(residual_in.shape, BF16),
-        in_specs=[scalars, scalars, anywhere, anywhere, anywhere],
+        in_specs=[anywhere] * 5,
         out_specs=pl.BlockSpec(memory_space=pltpu.VMEM),
         scratch_shapes=[
+            pltpu.SMEM(block_index.shape, I32),
+            pltpu.SMEM(block_sign.shape, I32),
             pltpu.VMEM((plane * HALVES, BLOCK // 2, BLOCK), BF16),
             pltpu.VMEM((depth, width), BF16),
             pltpu.VMEM(residual_in.shape, BF16),
             pltpu.VMEM((4 * BLOCK, depth), BF16),
-            pltpu.VMEM((4, 4, BLOCK, PW), F32),
-            pltpu.VMEM((4, 4, SHARE, PW), F32),
+            pltpu.VMEM((4, 2, 4 * SHARE, PW), F32),
+            pltpu.VMEM((4, 4 * SHARE, PW), F32),
             pltpu.VMEM((count, MROWS, 128), I16),
             pltpu.VMEM((count, MROWS, 128), I16),
-            pltpu.SemaphoreType.DMA((3,)),
+            pltpu.SemaphoreType.DMA((5,)),
             pltpu.SemaphoreType.DMA((n_sends,)),
             pltpu.SemaphoreType.DMA((NZ * 8,)),
             pltpu.SemaphoreType.DMA((8,)),
@@ -372,7 +378,7 @@
             pltpu.SemaphoreType.DMA((count,)),
         ],
         compiler_params=pltpu.CompilerParams(
-            collective_id=0, has_side_effects=True, vmem_limit_bytes=52 << 20
+            collective_id=0, has_side_effects=True, vmem_limit_bytes=63 << 20
         ),
         cost_estimate=pl.CostEstimate(
             flops=2 * 1024 * depth * width, bytes_accessed=depth * width * 2, transcendentals=0

time: 70.9 us -> 63.3 us (0.89)
  Pallas kernels: 66.7 us -> 61.6 us
  local copies, waits for them, and re-layouts: 3.95 us -> 1.67 us
    pallas_call x1, Pallas kernels: 66.7 us -> 61.6 us  [per_device(): pl.pallas_call(kernel, out_shape=jax.ShapeDtypeStruct(residual_in.shape,...]
    unnamed x9 -> x1, local copies, waits for them, and re-layouts: 3.95 us -> 1.67 us
where the time goes in v2:
time: 63.3 us; the launch traced here: 63.2 us
  Pallas kernels  61.6 us (97%)
  local copies, waits for them, and re-layouts  1.67 us (3%)
    pallas_call x1, Pallas kernels, per_device(): pl.pallas_call(kernel, out_shape=jax.ShapeDtypeStruct(residual_in.shape,...  61.6 us
    unnamed x1, local copies, waits for them, and re-layouts  1.67 us

profile of v2, /device:TPU:1, one launch (start us, length us, event | category | flops | bytes accessed | tf_op | source)
XLA Modules:
  0.0 63.2 jit_solution(13235154211347657884)
XLA Ops:
  0.0 61.6 %shard_map.55 = bf16[64,2048]{1,0:T(8,128)(2,1)} custom-call(s32[8,256]{1,0:T(8,128)} %index_hbm.1, s32[8,256]{1,0:T(8,128)} %sign_hbm.1, bf16[8,64,128]{2,1,0:T(8,128)(2,1)} %bitcast.1, bf16[2048,2048]{1,0:T(8,128)(2,1)} %ovov_ref.1, bf16[64,2048]{1,0:T(8,128)(2,1)} %residual_ref.1), custom_call_target="tpu_custom_call" | custom-call | flops 8589934592 | bytes 8388608 | tf_op jit(solution)/shard_map/pallas_call | solution.py:356
  61.6 1.7 %copy.7 = bf16[64,2048]{1,0:T(8,128)(2,1)} copy(bf16[64,2048]{1,0:T(8,128)(2,1)} %shard_map.55) | data formatting | bytes 524288

commit v3 on v2

v3 whole, which is shorter than its diff:
```python
import math

import jax
import jax.numpy as jnp
from jax import lax
from jax.experimental import pallas as pl
from jax.experimental.pallas import tpu as pltpu
from jax.sharding import PartitionSpec as P

MESH = pl.DeviceIdType.MESH
F32 = jnp.float32
BF16 = jnp.bfloat16
I16 = jnp.int16
I32 = jnp.int32

NY, NX, NZ = 4, 4, 4
BLOCK = 128
HALVES = 8
SHARE = 64
STEPS = 64.0
TOP = 32000.0
LN2 = math.log(2.0)

GATHER_ORDER = (
    "e00", "z00", "z01", "x00", "x01", "z10", "n00", "z11", "x10", "x11", "e10", "z20",
    "z21", "x20", "x21", "n10", "e20", "z30", "z31", "x30", "n20", "x31", "n30", "f00",
    "f10", "f20", "f30",
)

UNITS = [(0, 0, 512), (0, 512, 512), (0, 1024, 512), (0, 1536, 512), (1, 0, 512), (1, 512, 512), (1, 1024, 512), (1, 1536, 512)]
ORDER = (
    "b0", "t0", "m0", "d1", "f0", "g0", "d2", "f1", "g1", "d3", "s0", "f2",
    "g2", "s1", "b1", "d4", "f3", "g3", "n0", "s2", "d5", "f4", "g4", "n1",
    "s3", "d6", "f5", "g5", "n2", "s4", "d7", "f6", "g6", "n3", "s5", "f7",
    "g7", "s6", "n4", "s7", "n5", "n6", "n7",
)


def places():
    table, row = {}, 0
    for u, (h, start, width) in enumerate(UNITS):
        for k in range(7 if h == 0 else 6):
            tiles = width // (128 if k == 6 else 256)
            table[u * 7 + k] = (row, tiles)
            row += SHARE * tiles + 16
    return table, row


PLACES, MESSAGE_ROWS = places()


def encode(tiles):
    split = [t.reshape(SHARE // 16, 16, 128) for t in tiles]
    top = jnp.max(jnp.abs(split[0]), axis=0)
    for t in split[1:]:
        top = jnp.maximum(top, jnp.max(jnp.abs(t), axis=0))
    code = jnp.ceil(jnp.log(jnp.maximum(top, 1e-30)) * (STEPS / LN2)) + 1.0
    inverse = jnp.exp(code * (-LN2 / STEPS)) * TOP
    values = [
        jnp.round(t * inverse[None]).astype(I32).astype(I16).reshape(SHARE, 128) for t in split
    ]
    return values, code.astype(I32).astype(I16)


def decode(ref, first, tiles, wanted):
    code = ref[pl.ds(first + SHARE * tiles, 16), :].astype(I32).astype(F32)
    scale = jnp.exp(code * (LN2 / STEPS)) * (1.0 / TOP)
    out = []
    for t in wanted:
        v = ref[pl.ds(first + t * SHARE, SHARE), :].astype(I32).astype(F32)
        out.append((v.reshape(SHARE // 16, 16, 128) * scale[None]).reshape(SHARE, 128))
    return out


def add(a, b):
    return [x + y for x, y in zip(a, b)]


def kernel(
    index_hbm, sign_hbm, packed_ref, ovov_ref, residual_ref, out_ref,
    index_ref, sign_ref, gath, ovov, resid, slab, acc, d2d, msend, mrecv,
    local_sem, gs, gr, ds, dr, ms, mr, entered,
):
    row = lax.axis_index("row")
    col = lax.axis_index("col")
    dep = lax.axis_index("depth")
    core = lax.rem(row, 2)
    y = lax.rem(row // 2, NY)
    zh = row // (2 * NY)

    def row_of(zh_, y_, core_):
        return (zh_ * NY + y_) * 2 + core_

    sibling = {"row": row_of(zh, y, 1 - core)}
    y_up = {"row": row_of(zh, lax.rem(y + 1, NY), core)}
    y_down = {"row": row_of(zh, lax.rem(y + NY - 1, NY), core)}
    z_far = {"row": row_of(1 - zh, y, core)}
    dep_up, dep_down = lax.rem(dep + 1, NX), lax.rem(dep + NX - 1, NX)
    dep_far = lax.rem(dep + 2, NX)
    x_up, x_down = {"depth": dep_up}, {"depth": dep_down}
    z_up, z_down = {"col": lax.rem(col + 1, NZ)}, {"col": lax.rem(col + NZ - 1, NZ)}
    ring_up = {"row": row_of(lax.rem(zh + (col + 1) // NZ, 2), y, core), **z_up}
    ring_down = {
        "row": row_of(lax.rem(zh + 1 + (col + NZ - 1) // NZ, 2), y, core), **z_down
    }

    def slot(c, d):
        return (c * NX + d) * HALVES

    mine = slot(col, dep)
    own_copy = pltpu.make_async_copy(packed_ref, gath.at[pl.ds(mine, HALVES)], local_sem.at[0])
    own_copy.start()
    index_copy = pltpu.make_async_copy(index_hbm, index_ref, local_sem.at[3])
    sign_copy = pltpu.make_async_copy(sign_hbm, sign_ref, local_sem.at[4])
    index_copy.start()
    sign_copy.start()
    res_copy = pltpu.make_async_copy(residual_ref, resid, local_sem.at[1])
    ovov_copy = pltpu.make_async_copy(ovov_ref, ovov, local_sem.at[2])
    ovov_copy.start()
    res_copy.start()

    barrier = pltpu.get_barrier_semaphore()
    peers = (sibling, y_up, y_down, x_up, x_down, ring_up, ring_down)
    for p in peers:
        pl.semaphore_signal(barrier, inc=1, device_id=p, device_id_type=MESH)
    pl.semaphore_wait(barrier, len(peers))
    own_copy.wait()

    def relay(first):
        if not first:
            pl.semaphore_wait(entered, 1)
        pl.semaphore_signal(entered, inc=1, device_id=ring_down, device_id_type=MESH)


    PIECE = HALVES // 2
    sends = {}
    can_up, can_down = col < NZ - 1, col > 0

    def guarded(cond, fn):
        if cond is None:
            fn()
        else:
            pl.when(cond)(fn)

    def both(a, b):
        return b if a is None else jnp.logical_and(a, b)

    def gather_copy(first, sem, number, target):
        part = gath.at[pl.ds(first, PIECE)]
        return pltpu.make_async_remote_copy(
            part, part, gs.at[number], gr.at[sem], device_id=target, device_id_type=MESH
        )

    def send(key, cond, first, sem, target):
        copy = gather_copy(first, sem, len(sends), target)
        sends[key] = [cond, copy, True]
        guarded(cond, copy.start)

    def sent(key):
        cond, copy, flying = sends[key]
        if flying:
            guarded(cond, copy.wait_send)
        sends[key][2] = False

    def arrive(cond, first, sem):
        guarded(cond, gather_copy(first, sem, 0, sibling).wait_recv)

    def rows_at(k):
        if k == 0:
            return [(0, None, col)]
        return [(-1, col >= k, col - k), (1, col + k < NZ, col + k)]

    def z_piece(k, h):
        for side, cond, j in rows_at(k):
            first, sem = slot(j, dep) + h * PIECE, j * 8 + h
            if k > 0:
                arrive(cond, first, sem)
            if side <= 0:
                send(("z", k, h, side, 1), both(cond, can_up), first, sem, z_up)
            if side >= 0:
                send(("z", k, h, side, -1), both(cond, can_down), first, sem, z_down)

    def x_piece(k, h):
        for side, cond, j in rows_at(k):
            send(("x", k, h, side, 1), cond, slot(j, dep) + h * PIECE, j * 8 + 2 + h, x_up)
            send(
                ("x", k, h, side, -1), cond, slot(j, dep) + (1 - h) * PIECE, j * 8 + 5 - h, x_down
            )

    def x_forward(k):
        for side, cond, j in rows_at(k):
            first = slot(j, dep_down)
            arrive(cond, first, j * 8 + 2)
            send(("n", k, 0, side, 1), cond, first, j * 8 + 6, x_up)
            first = slot(j, dep_up) + PIECE
            arrive(cond, first, j * 8 + 5)
            send(("n", k, 0, side, -1), cond, first, j * 8 + 7, x_down)

    def x_last(k):
        for side, cond, j in rows_at(k):
            arrive(cond, slot(j, dep_down) + PIECE, j * 8 + 3)
            arrive(cond, slot(j, dep_up), j * 8 + 4)
            arrive(cond, slot(j, dep_far), j * 8 + 6)
            arrive(cond, slot(j, dep_far) + PIECE, j * 8 + 7)

    def sent_all(kind, k, h):
        for key in sorted(sends):
            if key[:3] == (kind, k, h):
                sent(key)

    for what in GATHER_ORDER:
        k, h = int(what[1]), int(what[2])
        if what[0] == "z":
            z_piece(k, h)
        elif what[0] == "x":
            x_piece(k, h)
        elif what[0] == "n":
            x_forward(k)
        elif what[0] == "f":
            x_last(k)
        elif what[0] == "w":
            sent_all("z", k, h)
        elif what[0] == "v":
            sent_all("x", k, h)
        elif what[0] == "e":
            relay(k == 0)
    for key in sorted(sends):
        sent(key)
    pl.semaphore_wait(entered, 1)
    ovov_copy.wait()
    index_copy.wait()
    sign_copy.wait()

    def block_row(h, i):
        yy = lax.rem(y + (2, 1, NY - 1, 0)[i], NY)
        return ((1 - zh) if h == 0 else zh) * NY + yy

    blocks_per_row = ovov.shape[0] // BLOCK
    HALF = 4 * SHARE

    def build(h):
        for i in range(4):
            r = block_row(h, i)

            @pl.loop(0, blocks_per_row)
            def _(s):
                at = row * blocks_per_row + s
                p = lax.rem(index_ref[r, at], gath.shape[0] // 2)
                sign = sign_ref[r, at].astype(F32)
                there = pl.ds(pl.multiple_of(s * BLOCK, BLOCK), BLOCK)
                for part, c in ((0, 1 - core), (1, core)):
                    tile = gath[2 * p + c]
                    slab[h, pl.ds(part * HALF + i * SHARE, SHARE), there] = (
                        tile.astype(F32) * sign
                    ).astype(BF16)

    core_copies = {}

    def multiply(u, parts):
        h, start, width = UNITS[u]
        rows = pl.ds(parts[0] * HALF, len(parts) * HALF)
        columns = pl.ds(start, width)
        acc[h, rows, columns] = jnp.dot(
            slab[h, rows, :], ovov[:, columns], preferred_element_type=F32
        )
        if 0 not in parts:
            return
        for w in range(2):
            rows = pl.ds(w * 2 * SHARE, 2 * SHARE)
            copy = pltpu.make_async_remote_copy(
                acc.at[h, rows, columns],
                d2d.at[h, rows, columns],
                ds.at[u * 2 + w],
                dr.at[u * 2 + w],
                device_id=sibling,
                device_id_type=MESH,
            )
            copy.start()
            core_copies[u, w] = copy

    def summed(u, i, half):
        h, start, width = UNITS[u]
        rows = pl.ds(i * SHARE, SHARE)
        out = []
        for t in range(width // 256):
            at = pl.ds(start + half * (width // 2) + t * 128, 128)
            out.append(acc[h, pl.ds(HALF + i * SHARE, SHARE), at] + d2d[h, rows, at])
        return out

    messages = {}

    def message_copy(number, target):
        first, tiles = PLACES[number]
        part = pl.ds(first, SHARE * tiles + 16)
        return pltpu.make_async_remote_copy(
            msend.at[part], mrecv.at[part], ms.at[number], mr.at[number],
            device_id=target, device_id_type=MESH,
        )

    def post(number, tiles, target):
        values, code = encode(tiles)
        first, count = PLACES[number]
        for t in range(count):
            msend[pl.ds(first + t * SHARE, SHARE), :] = values[t]
        msend[pl.ds(first + count * SHARE, 16), :] = code
        copy = message_copy(number, target)
        copy.start()
        messages[number] = copy

    def fetch(number):
        message_copy(number, sibling).wait_recv()
        first, count = PLACES[number]
        return decode(mrecv, first, count, range(count))

    A, B = 0, 1
    def first_sends(u):
        core_copies[u, 0].wait_recv()
        post(u * 7 + 0, summed(u, 0, A), y_up)
        post(u * 7 + 1, summed(u, 0, B), y_down)

    def near_sends(u):
        post(u * 7 + 2, summed(u, 1, B), y_up)
        core_copies[u, 1].wait_recv()
        post(u * 7 + 3, summed(u, 2, A), y_down)

    def second_sends(u):
        post(u * 7 + 4, add(summed(u, 1, A), fetch(u * 7 + 0)), y_up)
        post(u * 7 + 5, add(summed(u, 2, B), fetch(u * 7 + 1)), y_down)

    z_came = set()

    def z_tile(column):
        for u, (h, start, width) in enumerate(UNITS):
            if h == 0 and start <= column < start + width:
                number = u * 7 + 6
                if number not in z_came:
                    message_copy(number, sibling).wait_recv()
                    z_came.add(number)
                first, count = PLACES[number]
                return decode(mrecv, first, count, [(column - start) // 128])[0]

    def finish(u):
        h, start, width = UNITS[u]
        totals = []
        for half, direct, carried in ((A, 3, 4), (B, 2, 5)):
            totals += add(add(summed(u, 3, half), fetch(u * 7 + direct)), fetch(u * 7 + carried))
        if h == 0:
            post(u * 7 + 6, totals, z_far)
            return
        for t, total in enumerate(totals):
            column = start + t * 128
            at = pl.ds(column, 128)
            out_ref[:, at] = (resid[:, at].astype(F32) + (total + z_tile(column))).astype(BF16)

    def dots(u):
        multiply(u, (0, 1))

    def dots_theirs(u):
        multiply(u, (0,))

    def dots_mine(u):
        multiply(u, (1,))

    res_copy.wait()
    does = {
        "b": build, "t": dots_theirs, "m": dots_mine, "d": dots, "f": first_sends, "g": near_sends, "s": second_sends,
        "n": finish,
    }
    for what in ORDER:
        does[what[0]](int(what[1:]))

    for key in sorted(core_copies):
        core_copies[key].wait_send()
    for number in sorted(messages):
        messages[number].wait_send()


def per_device(packed, block_index, block_sign, ovov, residual_in):
    share, depth, width = packed.shape[0], ovov.shape[0], ovov.shape[1]
    plane = NZ * NX
    count = 7 * len(UNITS)
    n_sends = 64
    anywhere = pl.BlockSpec(memory_space=pl.ANY)
    return pl.pallas_call(
        kernel,
        out_shape=jax.ShapeDtypeStruct(residual_in.shape, BF16),
        in_specs=[anywhere] * 5,
        out_specs=pl.BlockSpec(memory_space=pltpu.VMEM),
        scratch_shapes=[
            pltpu.SMEM(block_index.shape, I32),
            pltpu.SMEM(block_sign.shape, I32),
            pltpu.VMEM((plane * HALVES, BLOCK // 2, BLOCK), BF16),
            pltpu.VMEM((depth, width), BF16),
            pltpu.VMEM(residual_in.shape, BF16),
            pltpu.VMEM((2, 4 * BLOCK, depth), BF16),
            pltpu.VMEM((2, 8 * SHARE, width), F32),
            pltpu.VMEM((2, 4 * SHARE, width), F32),
            pltpu.VMEM((MESSAGE_ROWS, 128), I16),
            pltpu.VMEM((MESSAGE_ROWS, 128), I16),
            pltpu.SemaphoreType.DMA((5,)),
            pltpu.SemaphoreType.DMA((n_sends,)),
            pltpu.SemaphoreType.DMA((NZ * 8,)),
            pltpu.SemaphoreType.DMA((2 * len(UNITS),)),
            pltpu.SemaphoreType.DMA((2 * len(UNITS),)),
            pltpu.SemaphoreType.DMA((count,)),
            pltpu.SemaphoreType.DMA((count,)),
            pltpu.SemaphoreType.REGULAR,
        ],
        compiler_params=pltpu.CompilerParams(
            collective_id=0, has_side_effects=True, vmem_limit_bytes=63 << 20
        ),
        cost_estimate=pl.CostEstimate(
            flops=2 * 1024 * depth * width, bytes_accessed=depth * width * 2, transcendentals=0
        ),
    )(
        block_index,
        block_sign,
        packed.reshape(share * 2, BLOCK // 2, BLOCK),
        ovov,
        residual_in,
    )


def solution(mesh):
    in_specs = (
        P(("row", "col", "depth"), None, None),
        P(),
        P(),
        P("row", ("col", "depth")),
        P("row", ("col", "depth")),
    )
    out_specs = P("row", ("col", "depth"))
    return jax.shard_map(
        per_device, mesh=mesh, in_specs=in_specs, out_specs=out_specs, check_vma=False
    )
```

time: 63.3 us -> 61.2 us (0.967)
  Pallas kernels: 61.6 us -> 59 us
    pallas_call x1, Pallas kernels: 61.6 us -> 59 us  [per_device(): pl.pallas_call(kernel, out_shape=jax.ShapeDtypeStruct(residual_in.shape,...]
where the time goes in v3:
time: 61.2 us; the launch traced here: 60.7 us
  Pallas kernels  59 us (96%)
  local copies, waits for them, and re-layouts  1.67 us (3%)
    pallas_call x1, Pallas kernels, per_device(): pl.pallas_call(kernel, out_shape=jax.ShapeDtypeStruct(residual_in.shape,...  59 us
    unnamed x1, local copies, waits for them, and re-layouts  1.67 us

profile of v3, /device:TPU:1, one launch (start us, length us, event | category | flops | bytes accessed | tf_op | source)
XLA Modules:
  0.0 60.7 jit_solution(11143603379315646707)
XLA Ops:
  0.0 59.0 %shard_map.55 = bf16[64,2048]{1,0:T(8,128)(2,1)} custom-call(s32[8,256]{1,0:T(8,128)} %index_hbm.1, s32[8,256]{1,0:T(8,128)} %sign_hbm.1, bf16[8,64,128]{2,1,0:T(8,128)(2,1)} %bitcast.1, bf16[2048,2048]{1,0:T(8,128)(2,1)} %ovov_ref.1, bf16[64,2048]{1,0:T(8,128)(2,1)} %residual_ref.1), custom_call_target="tpu_custom_call" | custom-call | flops 8589934592 | bytes 8388608 | tf_op jit(solution)/shard_map/pallas_call | solution.py:384
  59.0 1.7 %copy.7 = bf16[64,2048]{1,0:T(8,128)(2,1)} copy(bf16[64,2048]{1,0:T(8,128)(2,1)} %shard_map.55) | data formatting | bytes 524288

commit v4 on v3

--- a/solution.py
+++ b/solution.py
@@ -29,9 +29,9 @@
 
 UNITS = [(0, 0, 512), (0, 512, 512), (0, 1024, 512), (0, 1536, 512), (1, 0, 512), (1, 512, 512), (1, 1024, 512), (1, 1536, 512)]
 ORDER = (
-    "b0", "t0", "m0", "d1", "f0", "g0", "d2", "f1", "g1", "d3", "s0", "f2",
-    "g2", "s1", "b1", "d4", "f3", "g3", "n0", "s2", "d5", "f4", "g4", "n1",
-    "s3", "d6", "f5", "g5", "n2", "s4", "d7", "f6", "g6", "n3", "s5", "f7",
+    "b0", "t0", "m0", "d1", "f0", "g0", "d2", "f1", "g1", "d3", "f2", "g2",
+    "s0", "b1", "d4", "f3", "g3", "s1", "d5", "n0", "s2", "f4", "g4", "d6",
+    "n1", "s3", "f5", "g5", "d7", "n2", "s4", "f6", "g6", "n3", "s5", "f7",
     "g7", "s6", "n4", "s7", "n5", "n6", "n7",
 )
 

time: 61.2 us -> 60.6 us (level)
  Pallas kernels: 59 us -> 58.2 us
    pallas_call x1, Pallas kernels: 59 us -> 58.2 us  [per_device(): pl.pallas_call(kernel, out_shape=jax.ShapeDtypeStruct(residual_in.shape,...]
where the time goes in v4:
time: 60.6 us; the launch traced here: 59.9 us
  Pallas kernels  58.2 us (96%)
  local copies, waits for them, and re-layouts  1.67 us (3%)
    pallas_call x1, Pallas kernels, per_device(): pl.pallas_call(kernel, out_shape=jax.ShapeDtypeStruct(residual_in.shape,...  58.2 us
    unnamed x1, local copies, waits for them, and re-layouts  1.67 us

profile of v4, /device:TPU:1, one launch (start us, length us, event | category | flops | bytes accessed | tf_op | source)
XLA Modules:
  0.0 59.9 jit_solution(13820342508723124772)
XLA Ops:
  0.0 58.2 %shard_map.55 = bf16[64,2048]{1,0:T(8,128)(2,1)} custom-call(s32[8,256]{1,0:T(8,128)} %index_hbm.1, s32[8,256]{1,0:T(8,128)} %sign_hbm.1, bf16[8,64,128]{2,1,0:T(8,128)(2,1)} %bitcast.1, bf16[2048,2048]{1,0:T(8,128)(2,1)} %ovov_ref.1, bf16[64,2048]{1,0:T(8,128)(2,1)} %residual_ref.1), custom_call_target="tpu_custom_call" | custom-call | flops 8589934592 | bytes 8388608 | tf_op jit(solution)/shard_map/pallas_call | solution.py:384
  58.3 1.7 %copy.7 = bf16[64,2048]{1,0:T(8,128)(2,1)} copy(bf16[64,2048]{1,0:T(8,128)(2,1)} %shard_map.55) | data formatting | bytes 524288

commit v5 on v4

--- a/solution.py
+++ b/solution.py
@@ -224,9 +224,6 @@
             sent_all("x", k, h)
         elif what[0] == "e":
             relay(k == 0)
-    for key in sorted(sends):
-        sent(key)
-    pl.semaphore_wait(entered, 1)
     ovov_copy.wait()
     index_copy.wait()
     sign_copy.wait()
@@ -367,8 +364,12 @@
         "n": finish,
     }
     for what in ORDER:
+        if what == "n0":
+            pl.semaphore_wait(entered, 1)
         does[what[0]](int(what[1:]))
 
+    for key in sorted(sends):
+        sent(key)
     for key in sorted(core_copies):
         core_copies[key].wait_send()
     for number in sorted(messages):

time: 60.6 us -> 60.6 us (level)
  no operation moved by 1% of the time
where the time goes in v5:
time: 60.6 us; the launch traced here: 59.9 us
  Pallas kernels  58.3 us (96%)
  local copies, waits for them, and re-layouts  1.67 us (3%)
    pallas_call x1, Pallas kernels, per_device(): pl.pallas_call(kernel, out_shape=jax.ShapeDtypeStruct(residual_in.shape,...  58.3 us
    unnamed x1, local copies, waits for them, and re-layouts  1.67 us

profile of v5, /device:TPU:1, one launch (start us, length us, event | category | flops | bytes accessed | tf_op | source)
XLA Modules:
  0.0 59.9 jit_solution(12081914855531021468)
XLA Ops:
  0.0 58.3 %shard_map.55 = bf16[64,2048]{1,0:T(8,128)(2,1)} custom-call(s32[8,256]{1,0:T(8,128)} %index_hbm.1, s32[8,256]{1,0:T(8,128)} %sign_hbm.1, bf16[8,64,128]{2,1,0:T(8,128)(2,1)} %bitcast.1, bf16[2048,2048]{1,0:T(8,128)(2,1)} %ovov_ref.1, bf16[64,2048]{1,0:T(8,128)(2,1)} %residual_ref.1), custom_call_target="tpu_custom_call" | custom-call | flops 8589934592 | bytes 8388608 | tf_op jit(solution)/shard_map/pallas_call | solution.py:385
  58.3 1.7 %copy.7 = bf16[64,2048]{1,0:T(8,128)(2,1)} copy(bf16[64,2048]{1,0:T(8,128)(2,1)} %shard_map.55) | data formatting | bytes 524288
